TPU v7x, 32 devices: a whole 2x2x4 slice. The times are simulated.
32 devices in a mesh: groups: 2 (over y), seq: 4 (over z), head: 4 (over x, core).
Axes of the slice: x: 2, y: 2, z: 4, core: 2. Of those that a mesh axis runs over, the one named last changes fastest.
Arguments:
- queries: bfloat16 [4096, 2048], P(('groups', 'seq'), 'head'), parts along dimension 0, may hold values from -6 to 6
- keys: bfloat16 [4096, 2048], P(('groups', 'seq'), 'head'), parts along dimension 0, may hold values from -6 to 6
- values: bfloat16 [4096, 2048], P(('groups', 'seq'), 'head'), parts along dimension 0, may hold values from -6 to 6
- cotangent: bfloat16 [4096, 2048], P(('groups', 'seq'), 'head'), parts along dimension 0, may hold values from -6 to 6
- cluster_ids: int32 [2048, 1], P(('groups', 'seq')), parts along dimension 0, may hold values from 0 to 7; in each aligned block of 256 rows (0 to 255, 256 to 511, ...) at most 96 rows name the same one
- centroids: float32 [8, 2048], P(None, 'head'), may hold values from -0.6 to 0.6
Outputs:
- attended: bfloat16 [4096, 2048], P(('groups', 'seq'), 'head'), parts along dimension 0
- grad_queries: bfloat16 [4096, 2048], P(('groups', 'seq'), 'head'), parts along dimension 0
- grad_keys: bfloat16 [4096, 2048], P(('groups', 'seq'), 'head'), parts along dimension 0
- grad_values: bfloat16 [4096, 2048], P(('groups', 'seq'), 'head'), parts along dimension 0
- new_centroids: float32 [16, 2048], P('groups', 'head'), parts along dimension 0
There are 2 independent parts, one for each index of `groups`. A program takes and returns all parts, laid end to end along the dimension named above; an argument that names none is the same for every part. Nothing has to cross between parts.
Inputs may be any that keep to these rules, and one draw needn't show every extreme that they name: `cluster_ids`: tokens 2m and 2m+1 take the cluster of pair m. Among the 256 pairs of one index of seq no cluster is named more than 96 times, and some cluster is named exactly that often; every cluster is named by some pair.
All inputs are finite; a program needn't handle non-finite values.
Results may differ from a plain program's by a relative error of at most 0.02.
Values may be sent and summed in bfloat16 or wider, within the bound.
A program may use at most 128 MiB of HBM per device.

v0:
```python
import math

import jax
import jax.numpy as jnp
from jax import lax
from jax.sharding import PartitionSpec as P

HD = 128


def dispatch(stacked, slot_index, clusters, sources, slot_size):
    stack_size, tokens, feature_width = stacked.shape
    buffer = jnp.zeros((stack_size, clusters * slot_size, feature_width), stacked.dtype)
    buffer = buffer.at[:, slot_index, :].set(stacked)
    return buffer.reshape(stack_size, clusters // sources, sources, slot_size, feature_width)


def to_rows(block_data, head_count):
    item_count, sources, slot_size, feature_width = block_data.shape
    return block_data.reshape(
        item_count, sources * slot_size, head_count, feature_width // head_count
    )


def from_rows(row_data, sources):
    item_count, row_count, head_count, head_size = row_data.shape
    return row_data.reshape(item_count, sources, row_count // sources, head_count * head_size)


def live_mask(tallies, slot_size):
    count_table = tallies[0].astype(jnp.float32)
    item_count, sources = count_table.shape
    slot_place = jnp.arange(slot_size, dtype=jnp.float32)
    validity = (slot_place[None, None, :] < count_table[:, :, None]).reshape(
        item_count, sources * slot_size
    )
    row_count = sources * slot_size
    row_ids = lax.broadcasted_iota(jnp.int32, (row_count, row_count), 0)
    col_ids = lax.broadcasted_iota(jnp.int32, (row_count, row_count), 1)
    allowed = (
        validity[:, :, None] & validity[:, None, :] & (col_ids <= row_ids)[None]
        | (col_ids == row_ids)[None]
    )
    return allowed[:, None]


def probabilities(query_rows, key_rows, allowed, score_scale):
    logits = (
        jnp.einsum("irhd,ichd->ihrc", query_rows, key_rows, preferred_element_type=jnp.float32)
        * score_scale
    )
    highest = jnp.max(jnp.where(allowed, logits, -jnp.inf), axis=3, keepdims=True)
    lifted = jnp.where(allowed, jnp.exp(logits - highest), 0.0)
    chances = lifted / jnp.sum(lifted, axis=3, keepdims=True)
    return (chances, chances.astype(jnp.bfloat16))


def attend(rounded, value_rows):
    mixed_rows = jnp.einsum(
        "ihrc,ichd->irhd", rounded, value_rows, preferred_element_type=jnp.float32
    )
    return mixed_rows.astype(jnp.bfloat16)


def differentiate(
    chances, rounded, query_rows, key_rows, value_rows, grad_rows, attended, score_scale
):
    out_dot = jnp.sum(grad_rows.astype(jnp.float32) * attended.astype(jnp.float32), axis=3)
    grad_values = jnp.einsum(
        "ihrc,irhd->ichd", rounded, grad_rows, preferred_element_type=jnp.float32
    )
    grad_prob = jnp.einsum(
        "irhd,ichd->ihrc", grad_rows, value_rows, preferred_element_type=jnp.float32
    )
    grad_score = (
        chances * (grad_prob - out_dot.transpose(0, 2, 1)[..., None]) * score_scale
    ).astype(jnp.bfloat16)
    grad_queries = jnp.einsum(
        "ihrc,ichd->irhd", grad_score, key_rows, preferred_element_type=jnp.float32
    )
    grad_keys = jnp.einsum(
        "ihrc,irhd->ichd", grad_score, query_rows, preferred_element_type=jnp.float32
    )
    return (
        grad_queries.astype(jnp.bfloat16),
        grad_keys.astype(jnp.bfloat16),
        grad_values.astype(jnp.bfloat16),
    )


def renew(centroids, totals, tallies, head_count):
    blended = 0.5 * centroids + 0.5 * totals / tallies[:, None]
    shaped = blended.reshape(blended.shape[0], head_count, -1)
    normed = shaped * lax.rsqrt(jnp.mean(shaped * shaped, axis=2, keepdims=True) + 1e-06)
    return normed.reshape(blended.shape)


def body(queries, keys, values, cotangent, cluster_ids, centroids):
    sources = lax.axis_size("seq")
    tokens, feature_width = queries.shape
    clusters = centroids.shape[0]
    owned_count = clusters // sources
    head_count = feature_width // HD
    slot_size = 2 * (3 * tokens // (2 * clusters))
    score_scale = 1.0 / math.sqrt(HD)
    token_cluster = jnp.repeat(cluster_ids[:, 0], 2)
    member = (token_cluster[:, None] == lax.broadcasted_iota(jnp.int32, (1, clusters), 1)).astype(
        jnp.bfloat16
    )
    row_ids = lax.broadcasted_iota(jnp.int32, (tokens, tokens), 0)
    col_ids = lax.broadcasted_iota(jnp.int32, (tokens, tokens), 1)
    earlier = (col_ids < row_ids).astype(jnp.bfloat16)
    before = jnp.dot(earlier, member, preferred_element_type=jnp.float32)
    ranking = jnp.sum(before * member, axis=1).astype(jnp.int32)
    owner_place = token_cluster // owned_count
    item_place = token_cluster % owned_count
    slot_index = (item_place * sources + owner_place) * slot_size + ranking
    local_counts = jnp.sum(member, axis=0, dtype=jnp.float32)
    sent_counts = local_counts.astype(jnp.bfloat16).reshape(sources, owned_count).T[None]
    outgoing = dispatch(
        jnp.stack([queries, keys, values]), slot_index, clusters, sources, slot_size
    )
    payload, tallies = (
        lax.all_to_all(outgoing, "seq", split_axis=2, concat_axis=2, tiled=True),
        lax.all_to_all(sent_counts, "seq", split_axis=2, concat_axis=2, tiled=True),
    )
    allowed = live_mask(tallies, slot_size)
    query_rows = to_rows(payload[0], head_count)
    key_rows = to_rows(payload[1], head_count)
    value_rows = to_rows(payload[2], head_count)
    chances, rounded = probabilities(query_rows, key_rows, allowed, score_scale)
    attended = attend(rounded, value_rows)
    owner_side = payload.shape[2]
    returned_out = lax.all_to_all(
        from_rows(attended, owner_side)[None], "seq", split_axis=2, concat_axis=2, tiled=True
    )
    grad_outgoing = dispatch(cotangent[None], slot_index, clusters, sources, slot_size)
    grad_payload = lax.all_to_all(grad_outgoing, "seq", split_axis=2, concat_axis=2, tiled=True)
    grad_rows = to_rows(grad_payload[0], head_count)
    grads = differentiate(
        chances, rounded, query_rows, key_rows, value_rows, grad_rows, attended, score_scale
    )
    grad_stack = jnp.stack([from_rows(part_rows, owner_side) for part_rows in grads])
    returned_grads = lax.all_to_all(grad_stack, "seq", split_axis=2, concat_axis=2, tiled=True)
    returned = jnp.concatenate([returned_out, returned_grads])
    gathered = returned.reshape(4, clusters * slot_size, feature_width)[:, slot_index, :]
    local_totals = lax.dot_general(
        member, queries, (((0,), (0,)), ((), ())), preferred_element_type=jnp.float32
    )
    totals, all_counts = (
        lax.psum(local_totals.astype(jnp.bfloat16), "seq").astype(jnp.float32),
        lax.psum(local_counts.astype(jnp.bfloat16), "seq").astype(jnp.float32),
    )
    new_centroids = renew(centroids, totals, all_counts, head_count)
    return (gathered[0], gathered[1], gathered[2], gathered[3], new_centroids)


def solution(mesh):
    in_specs = (
        P(("groups", "seq"), "head"),
        P(("groups", "seq"), "head"),
        P(("groups", "seq"), "head"),
        P(("groups", "seq"), "head"),
        P(("groups", "seq"), None),
        P(None, "head"),
    )
    out_specs = (
        P(("groups", "seq"), "head"),
        P(("groups", "seq"), "head"),
        P(("groups", "seq"), "head"),
        P(("groups", "seq"), "head"),
        P("groups", "head"),
    )
    return jax.shard_map(body, mesh=mesh, in_specs=in_specs, out_specs=out_specs, check_vma=False)
```

profile of v0, /device:TPU:0, one launch (start us, length us, event | category | flops | bytes accessed | tf_op | source)
XLA Modules:
  0.0 471.3 jit_solution(12325580666806688266)
XLA Ops:
  2.4 6.3 %all-to-all-start.1 = ((bf16[1,2,4]{1,0,2:T(2,128)(2,1)}), bf16[1,2,4]{1,0,2:T(2,128)(2,1)S(1)}, u32[]{:S(2)}, u32[]{:S(2)}) async-start(bf16[1,2,4]{1,0,2:T(2,128)(2,1)} %copy.104), calls=%async_computation.1 | async-start | bytes 4096 | tf_op jit(solution)/shard_map/all_to_all | solution.py:125
  14.1 5.0 %all-to-all-start.3 = ((bf16[1,2,4,192,512]{4,3,1,0,2:T(8,128)(2,1)}), bf16[1,2,4,192,512]{4,3,1,0,2:T(8,128)(2,1)}, u32[]{:S(2)}, u32[]{:S(2)}) async-start(bf16[1,2,4,192,512]{4,3,1,0,2:T(8,128)(2,1)} %copy.114), calls=%async_computation.3 | async-start | bytes 3145728 | tf_op jit(solution)/shard_map/all_to_all | solution.py:138
  24.8 53.6 %scatter_fusion = bf16[3,1536,512]{2,0,1:T(4,128)(2,1)} fusion(bf16[3,1536,512]{2,0,1:T(4,128)(2,1)} %broadcast_in_dim.46, s32[512]{0:T(512)S(1)} %bitcast.81, bf16[512,3,512]{2,1,0:T(4,128)(2,1)S(1)} %copy.100), kind=kCustom, calls=%fused_computation.1 | custom fusion | bytes 4720640 | tf_op jit(solution)/shard_map/scatter | solution.py:14
  78.4 6.3 %copy.101 = bf16[3,2,4,192,512]{4,3,1,0,2:T(8,128)(2,1)} copy(bf16[3,2,4,192,512]{4,0,3,2,1:T(4,128)(2,1)} %bitcast.68) | data formatting | bytes 9437184 | tf_op jit(solution)/shard_map/reshape | solution.py:15
  84.7 5.2 %all-to-all-start = ((bf16[3,2,4,192,512]{4,3,1,0,2:T(8,128)(2,1)}), bf16[3,2,4,192,512]{4,3,1,0,2:T(8,128)(2,1)}, u32[]{:S(2)}, u32[]{:S(2)}) async-start(bf16[3,2,4,192,512]{4,3,1,0,2:T(8,128)(2,1)} %copy.101), calls=%async_computation | async-start | bytes 9437184 | tf_op jit(solution)/shard_map/all_to_all | solution.py:124
  92.5 4.2 copy.150
  100.6 93.1 %all-to-all-done = bf16[3,2,4,192,512]{4,3,1,0,2:T(8,128)(2,1)} async-done(((bf16[3,2,4,192,512]{4,3,1,0,2:T(8,128)(2,1)}), bf16[3,2,4,192,512]{4,3,1,0,2:T(8,128)(2,1)}, u32[]{:S(2)}, u32[]{:S(2)}) %all-to-all-start) | async-done | bytes 4718624 | tf_op jit(solution)/shard_map/all_to_all | solution.py:124
  193.6 4.5 fusion.28
  202.3 4.7 reshape.253
  219.4 9.3 %fusion.31 = f32[2,4,768,768]{2,3,1,0:T(8,128)} fusion(bf16[2,768,4,128]{1,3,2,0:T(8,128)(2,1)} %reshape.253, bf16[2,768,4,128]{1,3,2,0:T(8,128)(2,1)S(1)} %reshape.254), kind=kOutput, calls=%fused_computation.67 | convolution fusion | flops 1207959552 | bytes 22020096 | tf_op jit(solution)/shard_map/irhd,ichd->ihrc/dot_general | solution.py:49
  228.7 16.2 %fusion.30 = (f32[2,4,768]{2,1,0:T(4,128)S(1)}, f32[2,4,768,768]{2,3,1,0:T(8,128)}) fusion(bf16[2,768,4,128]{1,3,2,0:T(8,128)(2,1)} %reshape.253, bf16[2,768,4,128]{1,3,2,0:T(8,128)(2,1)S(1)} %reshape.254, pred[2,768,768]{1,2,0:T(8,128)(4,1)} %and_or_fusion, f32[2,4,768,768]{2,3,1,0:T(8,128)} %fusion.31), kind=kOutput, calls=%fused_computation.66 | convolution fusion | flops 1236271872 | bytes 42098688 | tf_op jit(solution)/shard_map/sub | solution.py:53
  244.9 7.5 %fusion.8 = bf16[2,4,768,768]{2,3,1,0:T(8,128)(2,1)S(1)} fusion(f32[2,4,768,768]{2,3,1,0:T(8,128)} %get-tuple-element.15, f32[2,4,768]{2,1,0:T(4,128)S(1)} %get-tuple-element.14), kind=kLoop, calls=%fused_computation.14 | loop fusion | flops 9437184 | bytes 28336128 | tf_op jit(solution)/shard_map/convert_element_type | solution.py:55
  256.4 10.3 %multiply_convert_fusion = bf16[2,4,768,768]{2,3,1,0:T(8,128)(2,1)} fusion(f32[2,4,768]{2,1,0:T(4,128)S(1)} %bitcast.79, f32[2,4,768,768]{2,3,1,0:T(8,128)} %get-tuple-element.15, f32[2,4,768]{2,1,0:T(4,128)S(1)} %get-tuple-element.14, bf16[2,768,4,128]{1,3,2,0:T(8,128)(2,1)S(1)} %reshape.255, bf16[2,768,4,128]{3,2,1,0:T(4,128)(2,1)S(1)} %copy-done.2), kind=kOutput, calls=%fused_computation.4 | convolution fusion | flops 1231552512 | bytes 31506432 | tf_op jit(solution)/shard_map/irhd,ichd->ihrc/dot_general | solution.py:72
  266.8 5.3 %reshape.252 = bf16[1,2,4,192,512]{3,2,4,1,0:T(4,128)(2,1)} reshape(bf16[2,768,4,128]{1,3,2,0:T(8,128)(2,1)} %get-tuple-element.17) | data formatting | bytes 3145728 | tf_op jit(solution)/shard_map/broadcast_in_dim;reshape | solution.py:135
  272.1 4.3 copy.113
  276.3 4.3 all-to-all-start.2
  280.7 8.0 %fusion.14 = bf16[2,768,4,128]{1,3,2,0:T(8,128)(2,1)} fusion(bf16[2,768,4,128]{1,3,2,0:T(8,128)(2,1)S(1)} %reshape.255, bf16[2,4,768,768]{2,3,1,0:T(8,128)(2,1)} %copy-done), kind=kOutput, calls=%fused_computation.29 | convolution fusion | flops 1208745984 | bytes 12582912 | tf_op jit(solution)/shard_map/ihrc,irhd->ichd/dot_general | solution.py:69
  296.2 8.0 %fusion.13 = bf16[2,768,4,128]{1,3,2,0:T(8,128)(2,1)} fusion(bf16[2,768,4,128]{1,3,2,0:T(8,128)(2,1)S(1)} %copy-done.1, bf16[2,4,768,768]{2,3,1,0:T(8,128)(2,1)} %multiply_convert_fusion), kind=kOutput, calls=%fused_computation.28 | convolution fusion | flops 1208745984 | bytes 12582912 | tf_op jit(solution)/shard_map/ihrc,irhd->ichd/dot_general | solution.py:81
  308.9 5.2 %fusion.12 = bf16[2,768,4,128]{1,3,2,0:T(8,128)(2,1)S(1)} fusion(bf16[2,768,4,128]{1,3,2,0:T(8,128)(2,1)S(1)} %reshape.254, bf16[2,4,768,768]{2,3,1,0:T(8,128)(2,1)} %multiply_convert_fusion), kind=kOutput, calls=%fused_computation.27 | convolution fusion | flops 1208745984 | bytes 12582912 | tf_op jit(solution)/shard_map/ihrc,ichd->irhd/dot_general | solution.py:78
  324.2 5.2 %all-to-all-start.4 = ((bf16[3,2,4,192,512]{4,3,1,0,2:T(8,128)(2,1)}), bf16[3,2,4,192,512]{4,3,1,0,2:T(8,128)(2,1)}, u32[]{:S(2)}, u32[]{:S(2)}) async-start(bf16[3,2,4,192,512]{4,3,1,0,2:T(8,128)(2,1)} %copy.129), calls=%async_computation.4 | async-start | bytes 9437184 | tf_op jit(solution)/shard_map/all_to_all | solution.py:144
  329.6 81.9 %all-reduce = (bf16[8]{0:T(256)(128)(2,1)S(1)}, bf16[8,512]{1,0:T(8,128)(2,1)S(1)}) all-reduce(bf16[8]{0:T(256)(128)(2,1)S(1)} %fusion.21, bf16[8,512]{1,0:T(8,128)(2,1)S(1)} %convolution_convert_fusion.4), channel_id=1, replica_groups=mesh['groups'=2,'seq'=4,'head'=4] {'seq'}, use_global_device_ids=true, to_apply=%region_8.9 | all-reduce | flops 4104 | bytes 16416 | tf_op jit(solution)/shard_map/psum | solution.py:152
  412.3 21.5 %all-to-all-done.4 = bf16[3,2,4,192,512]{4,3,1,0,2:T(8,128)(2,1)} async-done(((bf16[3,2,4,192,512]{4,3,1,0,2:T(8,128)(2,1)}), bf16[3,2,4,192,512]{4,3,1,0,2:T(8,128)(2,1)}, u32[]{:S(2)}, u32[]{:S(2)}) %all-to-all-start.4) | async-done | bytes 4718624 | tf_op jit(solution)/shard_map/all_to_all | solution.py:144
  437.9 20.8 %copy.132 = bf16[4,1536,512]{2,0,1:T(4,128)(2,1)} copy(bf16[4,1536,512]{2,1,0:T(8,128)(2,1)S(1)} %bitcast.69) | data formatting | bytes 12582912 | tf_op jit(solution)/shard_map/reshape | solution.py:146
  458.7 5.4 %gather_fusion = bf16[512,4,512]{2,1,0:T(4,128)(2,1)S(1)} fusion(bf16[4,1536,512]{2,0,1:T(4,128)(2,1)} %copy.132, s32[1024]{0:T(1024)S(1)} %pad_clamp_fusion), kind=kCustom, calls=%fused_computation | custom fusion | bytes 4196352 | tf_op jit(solution)/shard_map/gather | solution.py:146
  (74 shorter events, 74.1 us)
Async XLA Ops:
  2.4 11.8 %all-to-all-start.1 = ((bf16[1,2,4]{1,0,2:T(2,128)(2,1)}), bf16[1,2,4]{1,0,2:T(2,128)(2,1)S(1)}, u32[]{:S(2)}, u32[]{:S(2)}) async-start(bf16[1,2,4]{1,0,2:T(2,128)(2,1)} %copy.104), calls=%async_computation.1 | async-start | bytes 4096 | tf_op jit(solution)/shard_map/all_to_all | solution.py:125
  13.9 5.2 %copy-start.5 = (bf16[512,512]{1,0:T(8,128)(2,1)S(1)}, bf16[512,512]{1,0:T(8,128)(2,1)}, u32[]{:S(2)}) copy-start(bf16[512,512]{1,0:T(8,128)(2,1)} %param.6) | copy-start | bytes 1572868
  13.9 5.2 %copy-start.7 = (bf16[512,512]{1,0:T(8,128)(2,1)S(1)}, bf16[512,512]{1,0:T(8,128)(2,1)}, u32[]{:S(2)}) copy-start(bf16[512,512]{1,0:T(8,128)(2,1)} %param.8) | copy-start | bytes 1572868
  13.9 5.3 %copy-start.8 = (bf16[512,512]{1,0:T(8,128)(2,1)S(1)}, bf16[512,512]{1,0:T(8,128)(2,1)}, u32[]{:S(2)}) copy-start(bf16[512,512]{1,0:T(8,128)(2,1)} %param.7) | copy-start | bytes 1572868
  14.1 70.5 %all-to-all-start.3 = ((bf16[1,2,4,192,512]{4,3,1,0,2:T(8,128)(2,1)}), bf16[1,2,4,192,512]{4,3,1,0,2:T(8,128)(2,1)}, u32[]{:S(2)}, u32[]{:S(2)}) async-start(bf16[1,2,4,192,512]{4,3,1,0,2:T(8,128)(2,1)} %copy.114), calls=%async_computation.3 | async-start | bytes 3145728 | tf_op jit(solution)/shard_map/all_to_all | solution.py:138
  84.7 109.0 %all-to-all-start = ((bf16[3,2,4,192,512]{4,3,1,0,2:T(8,128)(2,1)}), bf16[3,2,4,192,512]{4,3,1,0,2:T(8,128)(2,1)}, u32[]{:S(2)}, u32[]{:S(2)}) async-start(bf16[3,2,4,192,512]{4,3,1,0,2:T(8,128)(2,1)} %copy.101), calls=%async_computation | async-start | bytes 9437184 | tf_op jit(solution)/shard_map/all_to_all | solution.py:124
  244.9 7.5 %copy-start.2 = (bf16[2,768,4,128]{3,2,1,0:T(4,128)(2,1)S(1)}, bf16[2,768,4,128]{3,2,1,0:T(4,128)(2,1)}, u32[]{:S(2)}) copy-start(bf16[2,768,4,128]{3,2,1,0:T(4,128)(2,1)} %reshape_squeeze.12) | copy-start | bytes 4718596
  252.4 4.0 copy-start
  276.3 47.9 %all-to-all-start.2 = ((bf16[1,2,4,192,512]{4,3,1,0,2:T(8,128)(2,1)}), bf16[1,2,4,192,512]{4,3,1,0,2:T(8,128)(2,1)}, u32[]{:S(2)}, u32[]{:S(2)}) async-start(bf16[1,2,4,192,512]{4,3,1,0,2:T(8,128)(2,1)} %copy.113), calls=%async_computation.2 | async-start | bytes 3145728 | tf_op jit(solution)/shard_map/all_to_all | solution.py:134
  292.4 3.8 copy-start.1
  316.3 3.8 copy-start.3
  316.3 3.8 copy-start.4
  324.2 5.2 %copy-start.6 = (bf16[512,512]{1,0:T(8,128)(2,1)S(1)}, bf16[512,512]{1,0:T(8,128)(2,1)}, u32[]{:S(2)}) copy-start(bf16[512,512]{1,0:T(8,128)(2,1)} %param.6) | copy-start | bytes 1572868
  324.2 87.3 %copy-start.9 = (f32[8,512]{1,0:T(8,128)S(1)}, f32[8,512]{1,0:T(8,128)}, u32[]{:S(2)}) copy-start(f32[8,512]{1,0:T(8,128)} %param.11) | copy-start | bytes 49156
  324.2 109.6 %all-to-all-start.4 = ((bf16[3,2,4,192,512]{4,3,1,0,2:T(8,128)(2,1)}), bf16[3,2,4,192,512]{4,3,1,0,2:T(8,128)(2,1)}, u32[]{:S(2)}, u32[]{:S(2)}) async-start(bf16[3,2,4,192,512]{4,3,1,0,2:T(8,128)(2,1)} %copy.129), calls=%async_computation.4 | async-start | bytes 9437184 | tf_op jit(solution)/shard_map/all_to_all | solution.py:144
where the time goes:
time: 480 us; the launch traced here: 471 us
  local copies, waits for them, and re-layouts  170 us (35%)
  waiting for transfers between devices  115 us (24%)
  blocking collectives  81.9 us (17%)
  matrix products  60.7 us (13%)
  starting transfers between devices  26 us (5%)
  other arithmetic  16 us (3%)
    all_to_all x1, waiting for transfers between devices, body(): lax.all_to_all(outgoing, 'seq', split_axis=2, concat_axis=2, tiled=True)  93.1 us
    psum x1, blocking collectives, body(): lax.psum(local_counts.astype(jnp.bfloat16), 'seq').astype(jnp.float32)  81.9 us
    scatter x2, local copies, waits for them, and re-layouts, dispatch(): buffer = buffer.at[:, slot_index, :].set(stacked)  57 us
    another operation x7, local copies, waits for them, and re-layouts, to_rows(): block_data.reshape(item_count, sources * slot_size, head_count, feature_w...  26.7 us
    all_to_all x1, waiting for transfers between devices, body(): lax.all_to_all(grad_stack, 'seq', split_axis=2, concat_axis=2, tiled=True)  21.5 us
    reshape x1, local copies, waits for them, and re-layouts, body(): returned.reshape(4, clusters * slot_size, feature_width)[:, slot_index, :]  20.8 us
    sub x1, matrix products, probabilities(): lifted = jnp.where(allowed, jnp.exp(logits - highest), 0.0)  16.2 us
    another operation x4, local copies, waits for them, and re-layouts, body(): jnp.stack([from_rows(part_rows, owner_side) for part_rows in grads])  12 us
  transfers between devices with their start and end apart: 5, of which 3 were waited for; matrix products, arithmetic and copies ran while one was open for 27% of the time, Pallas kernels for 0%

commit v1 on v0

--- a/solution.py
+++ b/solution.py
@@ -1,11 +1,375 @@
+import functools
 import math
 
 import jax
 import jax.numpy as jnp
 from jax import lax
+from jax.experimental import pallas as pl
+from jax.experimental.pallas import tpu as pltpu
 from jax.sharding import PartitionSpec as P
 
 HD = 128
+LANES = 128
+MESH = pl.DeviceIdType.MESH
+FAR = 131072.0
+NT = (((1,), (1,)), ((), ()))
+
+
+def product(a, b):
+    return jnp.dot(a, b, preferred_element_type=jnp.float32)
+
+
+def product_nt(a, b):
+    return lax.dot_general(a, b, NT, preferred_element_type=jnp.float32)
+
+
+def dense_kernel(
+    n, clusters, tile,
+    q_hbm, k_hbm, v_hbm, g_hbm, ids_ref, cent_ref,
+    out_ref, dq_ref, dk_ref, dv_ref, newc_ref,
+    qbuf, kbuf, vbuf, gbuf, idbuf, totbuf, statbuf, member, apart,
+    m_ref, l_ref, d_ref, acc, acc2,
+    own_sem, up_send, up_recv, down_send, down_recv,
+    id_send, id_recv, tot_send, tot_recv, stat_send, stat_recv,
+):
+    tokens, width = q_hbm.shape
+    heads = width // HD
+    tiles = tokens // tile
+    scale = 1.0 / math.sqrt(HD)
+    fold = scale * math.log2(math.e)
+    z = lax.axis_index("seq")
+
+    barrier = pltpu.get_barrier_semaphore()
+    for d in range(1, n):
+        pl.semaphore_signal(
+            barrier, inc=1, device_id={"seq": lax.rem(z + d, n)}, device_id_type=MESH
+        )
+
+    up_bufs, down_bufs = (kbuf, vbuf), (qbuf, gbuf)
+    up_src, down_src = (k_hbm, v_hbm), (q_hbm, g_hbm)
+    own = [
+        pltpu.make_async_copy(src, buf.at[z], own_sem.at[at])
+        for at, (src, buf) in enumerate(zip(up_src + down_src, up_bufs + down_bufs))
+    ]
+    for copy in own:
+        copy.start()
+    idbuf[z] = ids_ref[...]
+
+    def up_copy(kind, age, target):
+        block = z - age
+        src = up_src[kind] if age == 0 else up_bufs[kind].at[block]
+        return pltpu.make_async_remote_copy(
+            src_ref=src, dst_ref=up_bufs[kind].at[block],
+            send_sem=up_send.at[kind, age], recv_sem=up_recv.at[kind, age],
+            device_id={"seq": target}, device_id_type=MESH,
+        )
+
+    def down_copy(kind, age, target):
+        block = z + age
+        src = down_src[kind] if age == 0 else down_bufs[kind].at[block]
+        return pltpu.make_async_remote_copy(
+            src_ref=src, dst_ref=down_bufs[kind].at[block],
+            send_sem=down_send.at[kind, age], recv_sem=down_recv.at[kind, age],
+            device_id={"seq": target}, device_id_type=MESH,
+        )
+
+    def landed(bufs, sems, kind, age, block, target):
+        pltpu.make_async_remote_copy(
+            src_ref=bufs[kind].at[block], dst_ref=bufs[kind].at[block],
+            send_sem=sems.at[kind, age], recv_sem=sems.at[kind, age],
+            device_id={"seq": target}, device_id_type=MESH,
+        ).wait_recv()
+
+    def small_copy(buf, send, recv, d, slot):
+        return pltpu.make_async_remote_copy(
+            src_ref=buf.at[slot], dst_ref=buf.at[slot],
+            send_sem=send.at[d - 1], recv_sem=recv.at[d - 1],
+            device_id={"seq": lax.rem(z + d, n)}, device_id_type=MESH,
+        )
+
+    pl.semaphore_wait(barrier, n - 1)
+    for d in range(1, n):
+        small_copy(idbuf, id_send, id_recv, d, z).start()
+    for kind in range(2):
+        @pl.when(z < n - 1)
+        def _():
+            up_copy(kind, 0, z + 1).start()
+
+        @pl.when(z > 0)
+        def _():
+            down_copy(kind, 0, z - 1).start()
+
+    def spread_ids(block):
+        row = idbuf[block][0:1, :]
+        one_hot = (
+            lax.broadcasted_iota(jnp.int32, (LANES, tokens), 0).astype(jnp.float32) == row
+        ).astype(jnp.float32)
+        turned = one_hot.T
+        member[block] = turned.astype(jnp.bfloat16)
+        apart[block] = ((turned - 1.0) * FAR).astype(jnp.bfloat16)
+        return jnp.sum(one_hot, axis=1, keepdims=True)[0:clusters], one_hot[0:clusters]
+
+    counts, own_hot = spread_ids(z)
+    for copy in own:
+        copy.wait()
+    totbuf[z] = product(own_hot.astype(jnp.bfloat16), qbuf[z])
+    for d in range(1, n):
+        small_copy(totbuf, tot_send, tot_recv, d, z).start()
+
+    def place(step):
+        h = step // tiles
+        r = step % tiles
+        return (
+            h,
+            r,
+            pl.ds(pl.multiple_of(r * tile, tile), tile),
+            pl.ds(pl.multiple_of(h * HD, HD), HD),
+        )
+
+    def later(r):
+        row = lax.broadcasted_iota(jnp.int32, (tile, tokens), 0) + r * tile
+        col = lax.broadcasted_iota(jnp.int32, (tile, tokens), 1)
+        return row, col
+
+    def row_scores(block, rows, cols):
+        left = jnp.concatenate([qbuf[z, rows, cols], member[z, rows, :]], axis=1)
+        right = jnp.concatenate([kbuf[block, :, cols], apart[block]], axis=1)
+        return product_nt(left, right) * fold
+
+    def forward(block, diagonal):
+        @pl.loop(0, heads * tiles)
+        def _(step):
+            h, r, rows, cols = place(step)
+            s = row_scores(block, rows, cols)
+            if diagonal:
+                row, col = later(r)
+                s = jnp.where(col > row, -FAR, s)
+                top = jnp.max(s, axis=1, keepdims=True)
+                p = jnp.exp2(s - top)
+                l_ref[h, rows, :] = jnp.sum(p, axis=1, keepdims=True)
+                acc[rows, cols] = product(p.astype(jnp.bfloat16), vbuf[block, :, cols])
+            else:
+                old = m_ref[h, rows, :]
+                top = jnp.maximum(old, jnp.max(s, axis=1, keepdims=True))
+                p = jnp.exp2(s - top)
+                shrink = jnp.exp2(old - top)
+                l_ref[h, rows, :] = l_ref[h, rows, :] * shrink + jnp.sum(p, axis=1, keepdims=True)
+                acc[rows, cols] = acc[rows, cols] * shrink + product(
+                    p.astype(jnp.bfloat16), vbuf[block, :, cols]
+                )
+            m_ref[h, rows, :] = top
+
+    def row_gradient(block, diagonal):
+        @pl.loop(0, heads * tiles)
+        def _(step):
+            h, r, rows, cols = place(step)
+            s = row_scores(block, rows, cols) - m_ref[h, rows, :]
+            if diagonal:
+                row, col = later(r)
+                s = jnp.where(col > row, -FAR, s)
+            p = jnp.exp2(s)
+            dp = product_nt(gbuf[z, rows, cols], vbuf[block, :, cols])
+            ds = (p * (dp - d_ref[h, rows, :]) * scale).astype(jnp.bfloat16)
+            change = product(ds, kbuf[block, :, cols])
+            if diagonal:
+                acc[rows, cols] = change
+            else:
+                acc[rows, cols] += change
+
+    def column_gradient(block, diagonal):
+        @pl.loop(0, heads * tiles)
+        def _(step):
+            h, r, rows, cols = place(step)
+            left = jnp.concatenate([kbuf[z, rows, cols], apart[z, rows, :]], axis=1)
+            right = jnp.concatenate([qbuf[block, :, cols], member[block]], axis=1)
+            s = product_nt(left, right) * fold - statbuf[block, pl.ds(h, 1), :]
+            if diagonal:
+                row, col = later(r)
+                s = jnp.where(row > col, -FAR, s)
+            p = jnp.exp2(s)
+            grad = gbuf[block, :, cols]
+            dv = product(p.astype(jnp.bfloat16), grad)
+            dp = product_nt(vbuf[z, rows, cols], grad)
+            ds = (p * (dp - statbuf[block, pl.ds(heads + h, 1), :]) * scale).astype(jnp.bfloat16)
+            dk = product(ds, qbuf[block, :, cols])
+            if diagonal:
+                acc2[0, rows, cols] = dv
+                acc2[1, rows, cols] = dk
+            else:
+                acc2[0, rows, cols] += dv
+                acc2[1, rows, cols] += dk
+
+    def finish_rows():
+        lane = lax.broadcasted_iota(jnp.int32, (tokens, LANES), 1)
+        table = jnp.zeros((tokens, LANES), jnp.float32)
+        for h in range(heads):
+            cols = slice(h * HD, (h + 1) * HD)
+            total = l_ref[h]
+            attended = (acc[:, cols] / total).astype(jnp.bfloat16)
+            out_ref[:, cols] = attended
+            dot = jnp.sum(
+                gbuf[z, :, cols].astype(jnp.float32) * attended.astype(jnp.float32),
+                axis=1, keepdims=True,
+            )
+            level = m_ref[h] + jnp.log2(total)
+            m_ref[h] = level
+            d_ref[h] = dot
+            table = jnp.where(lane == h, level, table)
+            table = jnp.where(lane == heads + h, dot, table)
+        statbuf[z] = table.T[0 : statbuf.shape[1]]
+
+    def stat_copy(d):
+        return pltpu.make_async_remote_copy(
+            src_ref=statbuf.at[z], dst_ref=statbuf.at[z],
+            send_sem=stat_send.at[d - 1], recv_sem=stat_recv.at[d - 1],
+            device_id={"seq": z - d}, device_id_type=MESH,
+        )
+
+    def complete():
+        finish_rows()
+        for d in range(1, n):
+            @pl.when(z >= d)
+            def _():
+                stat_copy(d).start()
+        row_gradient(z, True)
+
+        @pl.loop(1, z + 1)
+        def _(age):
+            row_gradient(z - age, False)
+
+        column_gradient(z, True)
+
+    def column_turn(g):
+        pltpu.make_async_remote_copy(
+            src_ref=statbuf.at[z + g], dst_ref=statbuf.at[z + g],
+            send_sem=stat_send.at[g - 1], recv_sem=stat_recv.at[g - 1],
+            device_id={"seq": z + g}, device_id_type=MESH,
+        ).wait_recv()
+        column_gradient(z + g, False)
+
+    forward(z, True)
+    for d in range(1, n):
+        source = lax.rem(z + n - d, n)
+        small_copy(idbuf, id_send, id_recv, d, source).wait_recv()
+        small_copy(totbuf, tot_send, tot_recv, d, source).wait_recv()
+        other, _ = spread_ids(source)
+        counts = counts + other
+    totals = totbuf[0]
+    for j in range(1, n):
+        totals = totals + totbuf[j]
+    blended = 0.5 * cent_ref[...] + 0.5 * totals / counts
+    for h in range(heads):
+        part = blended[:, h * HD : (h + 1) * HD]
+        newc_ref[:, h * HD : (h + 1) * HD] = part * lax.rsqrt(
+            jnp.mean(part * part, axis=1, keepdims=True) + 1e-06
+        )
+
+    pl.when(z == 0)(complete)
+    for g in range(1, n):
+        for kind in range(2):
+            @pl.when(z >= g)
+            def _():
+                landed(up_bufs, up_recv, kind, g - 1, z - g, z - 1)
+
+                @pl.when(z < n - 1)
+                def _():
+                    up_copy(kind, g, z + 1).start()
+
+            @pl.when(z + g < n)
+            def _():
+                landed(down_bufs, down_recv, kind, g - 1, z + g, z + 1)
+
+                @pl.when(z > 0)
+                def _():
+                    down_copy(kind, g, z - 1).start()
+
+        @pl.when(z >= g)
+        def _():
+            forward(z - g, False)
+
+        pl.when(z == g)(complete)
+
+        @pl.when(z == 0)
+        def _():
+            column_turn(g)
+    for g in range(1, n - 1):
+        @pl.when((z > 0) & (z + g < n))
+        def _():
+            column_turn(g)
+
+    dq_ref[...] = acc[...].astype(jnp.bfloat16)
+    dv_ref[...] = acc2[0].astype(jnp.bfloat16)
+    dk_ref[...] = acc2[1].astype(jnp.bfloat16)
+
+    for d in range(1, n):
+        small_copy(idbuf, id_send, id_recv, d, z).wait_send()
+        small_copy(totbuf, tot_send, tot_recv, d, z).wait_send()
+
+        @pl.when(z >= d)
+        def _():
+            stat_copy(d).wait_send()
+    for age in range(n - 1):
+        for kind in range(2):
+            @pl.when((z >= age) & (z < n - 1))
+            def _():
+                up_copy(kind, age, z + 1).wait_send()
+
+            @pl.when((z + age < n) & (z > 0))
+            def _():
+                down_copy(kind, age, z - 1).wait_send()
+
+
+def dense_body(queries, keys, values, cotangent, cluster_ids, centroids):
+    n = lax.axis_size("seq")
+    tokens, width = queries.shape
+    clusters = centroids.shape[0]
+    heads = width // HD
+    tile = min(256, tokens)
+    stat_rows = -(-2 * heads // 8) * 8
+    ids = jnp.broadcast_to(
+        jnp.repeat(cluster_ids[:, 0], 2).astype(jnp.float32)[None, :], (8, tokens)
+    )
+    block = (n, tokens, width)
+    act = jax.ShapeDtypeStruct((tokens, width), jnp.bfloat16)
+    vmem = pl.BlockSpec(memory_space=pltpu.VMEM)
+    hbm = pl.BlockSpec(memory_space=pl.ANY)
+    dma = pltpu.SemaphoreType.DMA
+    return pl.pallas_call(
+        functools.partial(dense_kernel, n, clusters, tile),
+        out_shape=[act] * 4 + [jax.ShapeDtypeStruct((clusters, width), jnp.float32)],
+        in_specs=[hbm] * 4 + [vmem] * 2,
+        out_specs=[vmem] * 5,
+        scratch_shapes=[
+            pltpu.VMEM(block, jnp.bfloat16),
+            pltpu.VMEM(block, jnp.bfloat16),
+            pltpu.VMEM(block, jnp.bfloat16),
+            pltpu.VMEM(block, jnp.bfloat16),
+            pltpu.VMEM((n, 8, tokens), jnp.float32),
+            pltpu.VMEM((n, clusters, width), jnp.float32),
+            pltpu.VMEM((n, stat_rows, tokens), jnp.float32),
+            pltpu.VMEM((n, tokens, LANES), jnp.bfloat16),
+            pltpu.VMEM((n, tokens, LANES), jnp.bfloat16),
+            pltpu.VMEM((heads, tokens, 1), jnp.float32),
+            pltpu.VMEM((heads, tokens, 1), jnp.float32),
+            pltpu.VMEM((heads, tokens, 1), jnp.float32),
+            pltpu.VMEM((tokens, width), jnp.float32),
+            pltpu.VMEM((2, tokens, width), jnp.float32),
+            dma((4,)),
+            dma((2, n - 1)),
+            dma((2, n - 1)),
+            dma((2, n - 1)),
+            dma((2, n - 1)),
+            dma((n - 1,)),
+            dma((n - 1,)),
+            dma((n - 1,)),
+            dma((n - 1,)),
+            dma((n - 1,)),
+            dma((n - 1,)),
+        ],
+        compiler_params=pltpu.CompilerParams(
+            collective_id=0, has_side_effects=True, vmem_limit_bytes=48 * 1024 * 1024
+        ),
+    )(queries, keys, values, cotangent, ids, centroids)
 
 
 def dispatch(stacked, slot_index, clusters, sources, slot_size):
@@ -95,7 +459,7 @@
     return normed.reshape(blended.shape)
 
 
-def body(queries, keys, values, cotangent, cluster_ids, centroids):
+def dispatch_body(queries, keys, values, cotangent, cluster_ids, centroids):
     sources = lax.axis_size("seq")
     tokens, feature_width = queries.shape
     clusters = centroids.shape[0]
@@ -155,6 +519,17 @@
     return (gathered[0], gathered[1], gathered[2], gathered[3], new_centroids)
 
 
+def body(queries, keys, values, cotangent, cluster_ids, centroids):
+    sources = lax.axis_size("seq")
+    tokens = queries.shape[0]
+    clusters = centroids.shape[0]
+    slot_size = 2 * (3 * tokens // (2 * clusters))
+    clustered_work = clusters // sources * (sources * slot_size) ** 2
+    dense_work = sources * tokens * tokens
+    chosen = dense_body if dense_work <= clustered_work else dispatch_body
+    return chosen(queries, keys, values, cotangent, cluster_ids, centroids)
+
+
 def solution(mesh):
     in_specs = (
         P(("groups", "seq"), "head"),

time: 480 us -> 112 us (0.23)
  the two profiles are of different devices: /device:TPU:0 before, /device:TPU:24 now
where the time goes in v1:
time: 112 us
  Pallas kernels  102 us (91%)
  local copies, waits for them, and re-layouts  8.88 us (8%)
    pallas_call x1, Pallas kernels, dense_body(): pl.pallas_call(functools.partial(dense_kernel, n, clusters, tile), out_sh...  102 us
    unnamed x15, local copies, waits for them, and re-layouts  8.65 us

profile of v1, /device:TPU:24, one launch (start us, length us, event | category | flops | bytes accessed | tf_op | source)
XLA Modules:
  0.0 112.1 jit_solution(17397512317870943192)
XLA Ops:
  0.6 0.7 convert_element_type.14
  1.3 0.1 broadcast_in_dim.4
  1.4 0.1 convert_element_type.16
  1.6 0.0 copy-start.4
  1.6 0.7 copy-done.4
  2.3 0.0 copy-start
  2.3 1.0 copy-done
  3.3 0.0 copy-start.1
  3.3 1.0 copy-done.1
  4.4 0.0 copy-start.2
  4.4 1.0 copy-done.2
  5.4 0.0 copy-start.3
  5.4 1.0 copy-done.3
  6.4 101.8 %shard_map.101 = (bf16[512,512]{1,0:T(8,128)(2,1)S(1)}, bf16[512,512]{1,0:T(8,128)(2,1)S(1)}, bf16[512,512]{1,0:T(8,128)(2,1)S(1)}, bf16[512,512]{1,0:T(8,128)(2,1)S(1)}, f32[8,512]{1,0:T(8,128)S(1)}) custom-call(bf16[512,512]{1,0:T(8,128)(2,1)S(1)} %copy-done, bf16[512,512]{1,0:T(8,128)(2,1)S(1)} %copy-done.1, bf16[512,512]{1,0:T(8,128)(2,1)S(1)} %copy-done.2, ...), custom_call_target="tpu_custom_call" | custom-call | tf_op jit(solution)/shard_map/pallas_call | solution.py:337
  108.3 0.8 copy.16
  109.1 0.8 copy.17
  109.9 0.8 copy.18
  110.7 0.8 copy.19
  111.5 0.6 copy.20
  (1 shorter events, 0.0 us)
Async XLA Ops:
  1.6 0.7 copy-start.4
  2.3 1.0 copy-start
  3.3 1.0 copy-start.1
  4.4 1.0 copy-start.2
  5.4 1.0 copy-start.3

commit v2 on v1

--- a/solution.py
+++ b/solution.py
@@ -13,6 +13,7 @@
 MESH = pl.DeviceIdType.MESH
 FAR = 131072.0
 NT = (((1,), (1,)), ((), ()))
+TN = (((0,), (0,)), ((), ()))
 
 
 def product(a, b):
@@ -27,10 +28,10 @@
     n, clusters, tile,
     q_hbm, k_hbm, v_hbm, g_hbm, ids_ref, cent_ref,
     out_ref, dq_ref, dk_ref, dv_ref, newc_ref,
-    qbuf, kbuf, vbuf, gbuf, idbuf, totbuf, statbuf, member, apart,
+    qbuf, kbuf, vbuf, gbuf, idbuf, totbuf, levbuf, statbuf, member, apart, kept_p, kept_d,
     m_ref, l_ref, d_ref, acc, acc2,
     own_sem, up_send, up_recv, down_send, down_recv,
-    id_send, id_recv, tot_send, tot_recv, stat_send, stat_recv,
+    id_send, id_recv, tot_send, tot_recv, lev_send, lev_recv, stat_send, stat_recv,
 ):
     tokens, width = q_hbm.shape
     heads = width // HD
@@ -90,14 +91,21 @@
     pl.semaphore_wait(barrier, n - 1)
     for d in range(1, n):
         small_copy(idbuf, id_send, id_recv, d, z).start()
-    for kind in range(2):
-        @pl.when(z < n - 1)
-        def _():
-            up_copy(kind, 0, z + 1).start()
-
-        @pl.when(z > 0)
-        def _():
-            down_copy(kind, 0, z - 1).start()
+    @pl.when(z < n - 1)
+    def _():
+        up_copy(0, 0, z + 1).start()
+
+    @pl.when(z > 0)
+    def _():
+        down_copy(0, 0, z - 1).start()
+
+    @pl.when(z == 0)
+    def _():
+        up_copy(1, 0, z + 1).start()
+
+    @pl.when(z == n - 1)
+    def _():
+        down_copy(1, 0, z - 1).start()
 
     def spread_ids(block):
         row = idbuf[block][0:1, :]
@@ -136,7 +144,10 @@
         right = jnp.concatenate([kbuf[block, :, cols], apart[block]], axis=1)
         return product_nt(left, right) * fold
 
-    def forward(block, diagonal):
+    def wide(h):
+        return pl.ds(pl.multiple_of(h * tokens, tokens), tokens)
+
+    def score(block, diagonal):
         @pl.loop(0, heads * tiles)
         def _(step):
             h, r, rows, cols = place(step)
@@ -145,109 +156,128 @@
                 row, col = later(r)
                 s = jnp.where(col > row, -FAR, s)
                 top = jnp.max(s, axis=1, keepdims=True)
-                p = jnp.exp2(s - top)
-                l_ref[h, rows, :] = jnp.sum(p, axis=1, keepdims=True)
-                acc[rows, cols] = product(p.astype(jnp.bfloat16), vbuf[block, :, cols])
+                l_ref[h, rows, :] = jnp.sum(jnp.exp2(s - top), axis=1, keepdims=True)
             else:
                 old = m_ref[h, rows, :]
                 top = jnp.maximum(old, jnp.max(s, axis=1, keepdims=True))
-                p = jnp.exp2(s - top)
-                shrink = jnp.exp2(old - top)
-                l_ref[h, rows, :] = l_ref[h, rows, :] * shrink + jnp.sum(p, axis=1, keepdims=True)
-                acc[rows, cols] = acc[rows, cols] * shrink + product(
-                    p.astype(jnp.bfloat16), vbuf[block, :, cols]
+                l_ref[h, rows, :] = l_ref[h, rows, :] * jnp.exp2(old - top) + jnp.sum(
+                    jnp.exp2(s - top), axis=1, keepdims=True
                 )
             m_ref[h, rows, :] = top
+            kept_p[block, rows, wide(h)] = s
+
+    def normalise(block):
+        @pl.loop(0, heads * tiles)
+        def _(step):
+            h, r, rows, cols = place(step)
+            kept_p[block, rows, wide(h)] = jnp.exp2(
+                kept_p[block, rows, wide(h)] - m_ref[h, rows, :]
+            )
+
+    def attend_block(block, diagonal):
+        @pl.loop(0, heads * tiles)
+        def _(step):
+            h, r, rows, cols = place(step)
+            value = vbuf[block, :, cols]
+            grad = gbuf[z, rows, cols]
+            p = kept_p[block, rows, wide(h)].astype(jnp.bfloat16)
+            change = product(p, value)
+            kept_d[block, rows, wide(h)] = product_nt(grad, value)
+            if diagonal:
+                acc[rows, cols] = change
+                acc2[0, :, cols] += lax.dot_general(
+                    p, grad, TN, preferred_element_type=jnp.float32
+                )
+            else:
+                acc[rows, cols] += change
 
     def row_gradient(block, diagonal):
         @pl.loop(0, heads * tiles)
         def _(step):
             h, r, rows, cols = place(step)
-            s = row_scores(block, rows, cols) - m_ref[h, rows, :]
-            if diagonal:
-                row, col = later(r)
-                s = jnp.where(col > row, -FAR, s)
-            p = jnp.exp2(s)
-            dp = product_nt(gbuf[z, rows, cols], vbuf[block, :, cols])
+            p = kept_p[block, rows, wide(h)]
+            dp = kept_d[block, rows, wide(h)]
             ds = (p * (dp - d_ref[h, rows, :]) * scale).astype(jnp.bfloat16)
             change = product(ds, kbuf[block, :, cols])
             if diagonal:
                 acc[rows, cols] = change
+                acc2[1, :, cols] += lax.dot_general(
+                    ds, qbuf[z, rows, cols], TN, preferred_element_type=jnp.float32
+                )
             else:
                 acc[rows, cols] += change
 
-    def column_gradient(block, diagonal):
+    def column_gradient(block):
         @pl.loop(0, heads * tiles)
         def _(step):
             h, r, rows, cols = place(step)
             left = jnp.concatenate([kbuf[z, rows, cols], apart[z, rows, :]], axis=1)
             right = jnp.concatenate([qbuf[block, :, cols], member[block]], axis=1)
-            s = product_nt(left, right) * fold - statbuf[block, pl.ds(h, 1), :]
-            if diagonal:
-                row, col = later(r)
-                s = jnp.where(row > col, -FAR, s)
+            s = product_nt(left, right) * fold - levbuf[block, pl.ds(h, 1), :]
             p = jnp.exp2(s)
             grad = gbuf[block, :, cols]
             dv = product(p.astype(jnp.bfloat16), grad)
             dp = product_nt(vbuf[z, rows, cols], grad)
-            ds = (p * (dp - statbuf[block, pl.ds(heads + h, 1), :]) * scale).astype(jnp.bfloat16)
+            ds = (p * (dp - statbuf[block, pl.ds(h, 1), :]) * scale).astype(jnp.bfloat16)
             dk = product(ds, qbuf[block, :, cols])
-            if diagonal:
-                acc2[0, rows, cols] = dv
-                acc2[1, rows, cols] = dk
-            else:
-                acc2[0, rows, cols] += dv
-                acc2[1, rows, cols] += dk
-
-    def finish_rows():
+            acc2[0, rows, cols] += dv
+            acc2[1, rows, cols] += dk
+
+    def down_small(buf, send, recv, d, slot, target):
+        return pltpu.make_async_remote_copy(
+            src_ref=buf.at[slot], dst_ref=buf.at[slot],
+            send_sem=send.at[d - 1], recv_sem=recv.at[d - 1],
+            device_id={"seq": target}, device_id_type=MESH,
+        )
+
+    def tell_lower(buf, send, recv):
+        for d in range(1, n):
+            @pl.when(z >= d)
+            def _():
+                down_small(buf, send, recv, d, z, z - d).start()
+
+    def finish_scores():
+        lane = lax.broadcasted_iota(jnp.int32, (tokens, LANES), 1)
+        table = jnp.zeros((tokens, LANES), jnp.float32)
+        for h in range(heads):
+            level = m_ref[h] + jnp.log2(l_ref[h])
+            m_ref[h] = level
+            table = jnp.where(lane == h, level, table)
+        levbuf[z] = table.T[0 : levbuf.shape[1]]
+        tell_lower(levbuf, lev_send, lev_recv)
+
+        @pl.loop(0, z + 1)
+        def _(age):
+            normalise(z - age)
+
+    def complete():
         lane = lax.broadcasted_iota(jnp.int32, (tokens, LANES), 1)
         table = jnp.zeros((tokens, LANES), jnp.float32)
         for h in range(heads):
             cols = slice(h * HD, (h + 1) * HD)
-            total = l_ref[h]
-            attended = (acc[:, cols] / total).astype(jnp.bfloat16)
+            attended = acc[:, cols].astype(jnp.bfloat16)
             out_ref[:, cols] = attended
             dot = jnp.sum(
                 gbuf[z, :, cols].astype(jnp.float32) * attended.astype(jnp.float32),
                 axis=1, keepdims=True,
             )
-            level = m_ref[h] + jnp.log2(total)
-            m_ref[h] = level
             d_ref[h] = dot
-            table = jnp.where(lane == h, level, table)
-            table = jnp.where(lane == heads + h, dot, table)
+            table = jnp.where(lane == h, dot, table)
         statbuf[z] = table.T[0 : statbuf.shape[1]]
-
-    def stat_copy(d):
-        return pltpu.make_async_remote_copy(
-            src_ref=statbuf.at[z], dst_ref=statbuf.at[z],
-            send_sem=stat_send.at[d - 1], recv_sem=stat_recv.at[d - 1],
-            device_id={"seq": z - d}, device_id_type=MESH,
-        )
-
-    def complete():
-        finish_rows()
-        for d in range(1, n):
-            @pl.when(z >= d)
-            def _():
-                stat_copy(d).start()
+        tell_lower(statbuf, stat_send, stat_recv)
         row_gradient(z, True)
 
         @pl.loop(1, z + 1)
         def _(age):
             row_gradient(z - age, False)
 
-        column_gradient(z, True)
-
     def column_turn(g):
-        pltpu.make_async_remote_copy(
-            src_ref=statbuf.at[z + g], dst_ref=statbuf.at[z + g],
-            send_sem=stat_send.at[g - 1], recv_sem=stat_recv.at[g - 1],
-            device_id={"seq": z + g}, device_id_type=MESH,
-        ).wait_recv()
-        column_gradient(z + g, False)
-
-    forward(z, True)
+        down_small(levbuf, lev_send, lev_recv, g, z + g, z + g).wait_recv()
+        down_small(statbuf, stat_send, stat_recv, g, z + g, z + g).wait_recv()
+        column_gradient(z + g)
+
+    acc2[...] = jnp.zeros_like(acc2)
+    score(z, True)
     for d in range(1, n):
         source = lax.rem(z + n - d, n)
         small_copy(idbuf, id_send, id_recv, d, source).wait_recv()
@@ -264,28 +294,50 @@
             jnp.mean(part * part, axis=1, keepdims=True) + 1e-06
         )
 
+    def pass_on(kind, g, seen_up, seen_down):
+        @pl.when(z >= g)
+        def _():
+            landed(up_bufs, up_recv, kind, g - 1, z - g, z - 1)
+
+            @pl.when(z < n - 1)
+            def _():
+                up_copy(kind, g, z + 1).start()
+
+        if seen_up:
+            @pl.when((z == g) & (z < n - 1))
+            def _():
+                up_copy(1, 0, z + 1).start()
+
+        @pl.when(z + g < n)
+        def _():
+            landed(down_bufs, down_recv, kind, g - 1, z + g, z + 1)
+
+            @pl.when(z > 0)
+            def _():
+                down_copy(kind, g, z - 1).start()
+
+        if seen_down:
+            @pl.when((z + g == n - 1) & (z > 0))
+            def _():
+                down_copy(1, 0, z - 1).start()
+
+    pl.when(z == 0)(finish_scores)
+    for g in range(1, n):
+        pass_on(0, g, True, True)
+
+        @pl.when(z >= g)
+        def _():
+            score(z - g, False)
+
+        pl.when(z == g)(finish_scores)
+    attend_block(z, True)
     pl.when(z == 0)(complete)
     for g in range(1, n):
-        for kind in range(2):
-            @pl.when(z >= g)
-            def _():
-                landed(up_bufs, up_recv, kind, g - 1, z - g, z - 1)
-
-                @pl.when(z < n - 1)
-                def _():
-                    up_copy(kind, g, z + 1).start()
-
-            @pl.when(z + g < n)
-            def _():
-                landed(down_bufs, down_recv, kind, g - 1, z + g, z + 1)
-
-                @pl.when(z > 0)
-                def _():
-                    down_copy(kind, g, z - 1).start()
+        pass_on(1, g, False, False)
 
         @pl.when(z >= g)
         def _():
-            forward(z - g, False)
+            attend_block(z - g, False)
 
         pl.when(z == g)(complete)
 
@@ -307,7 +359,8 @@
 
         @pl.when(z >= d)
         def _():
-            stat_copy(d).wait_send()
+            down_small(levbuf, lev_send, lev_recv, d, z, z - d).wait_send()
+            down_small(statbuf, stat_send, stat_recv, d, z, z - d).wait_send()
     for age in range(n - 1):
         for kind in range(2):
             @pl.when((z >= age) & (z < n - 1))
@@ -325,14 +378,14 @@
     clusters = centroids.shape[0]
     heads = width // HD
     tile = min(256, tokens)
-    stat_rows = -(-2 * heads // 8) * 8
+    stat_rows = -(-heads // 8) * 8
     ids = jnp.broadcast_to(
         jnp.repeat(cluster_ids[:, 0], 2).astype(jnp.float32)[None, :], (8, tokens)
     )
     block = (n, tokens, width)
     act = jax.ShapeDtypeStruct((tokens, width), jnp.bfloat16)
     vmem = pl.BlockSpec(memory_space=pltpu.VMEM)
-    hbm = pl.BlockSpec(memory_space=pl.ANY)
+    hbm = pl.BlockSpec(memory_space=pltpu.HBM)
     dma = pltpu.SemaphoreType.DMA
     return pl.pallas_call(
         functools.partial(dense_kernel, n, clusters, tile),
@@ -347,8 +400,11 @@
             pltpu.VMEM((n, 8, tokens), jnp.float32),
             pltpu.VMEM((n, clusters, width), jnp.float32),
             pltpu.VMEM((n, stat_rows, tokens), jnp.float32),
+            pltpu.VMEM((n, stat_rows, tokens), jnp.float32),
             pltpu.VMEM((n, tokens, LANES), jnp.bfloat16),
             pltpu.VMEM((n, tokens, LANES), jnp.bfloat16),
+            pltpu.VMEM((n, tokens, heads * tokens), jnp.float32),
+            pltpu.VMEM((n, tokens, heads * tokens), jnp.float32),
             pltpu.VMEM((heads, tokens, 1), jnp.float32),
             pltpu.VMEM((heads, tokens, 1), jnp.float32),
             pltpu.VMEM((heads, tokens, 1), jnp.float32),
@@ -365,9 +421,11 @@
             dma((n - 1,)),
             dma((n - 1,)),
             dma((n - 1,)),
+            dma((n - 1,)),
+            dma((n - 1,)),
         ],
         compiler_params=pltpu.CompilerParams(
-            collective_id=0, has_side_effects=True, vmem_limit_bytes=48 * 1024 * 1024
+            collective_id=0, has_side_effects=True, vmem_limit_bytes=60 * 1024 * 1024
         ),
     )(queries, keys, values, cotangent, ids, centroids)
 

time: 112 us -> 111 us (level)
  the two profiles are of different devices: /device:TPU:24 before, /device:TPU:0 now
where the time goes in v2:
time: 111 us
  Pallas kernels  103 us (93%)
  local copies, waits for them, and re-layouts  6.64 us (6%)
    pallas_call x1, Pallas kernels, dense_body(): pl.pallas_call(functools.partial(dense_kernel, n, clusters, tile), out_sh...  103 us
    unnamed x13, local copies, waits for them, and re-layouts  5.79 us

profile of v2, /device:TPU:0, one launch (start us, length us, event | category | flops | bytes accessed | tf_op | source)
XLA Modules:
  0.0 110.7 jit_solution(6798353477921147233)
XLA Ops:
  0.6 0.7 convert_element_type.14
  1.3 0.1 broadcast_in_dim.4
  1.4 0.1 convert_element_type.16
  1.6 0.6 broadcast_in_dim.10.ids_ref
  2.2 102.7 %shard_map.101 = (bf16[512,512]{1,0:T(8,128)(2,1)}, bf16[512,512]{1,0:T(8,128)(2,1)}, bf16[512,512]{1,0:T(8,128)(2,1)}, bf16[512,512]{1,0:T(8,128)(2,1)}, f32[8,512]{1,0:T(8,128)}) custom-call(bf16[512,512]{1,0:T(8,128)(2,1)} %q_hbm.1, bf16[512,512]{1,0:T(8,128)(2,1)} %k_hbm.1, bf16[512,512]{1,0:T(8,128)(2,1)} %v_hbm.1, bf16[512,512]{1,0:T(8,128)(2,1)} %g_hbm.1, ...), custom_call_target="tpu_custom_call" | custom-call | tf_op jit(solution)/shard_map/pallas_call | solution.py:390
  104.9 0.0 copy-start.2
  104.9 1.9 %copy.16 = bf16[512,512]{1,0:T(8,128)(2,1)} copy(bf16[512,512]{1,0:T(8,128)(2,1)} %get-tuple-element.10) | data formatting | bytes 1048576
  106.8 0.0 copy-done.2
  106.8 0.0 copy-start.1
  106.8 0.8 copy.17
  107.6 0.4 copy-done.1
  108.1 0.0 copy-start
  108.1 0.8 copy.18
  108.9 0.4 copy-done
  109.3 0.0 copy-start.3
  109.3 0.8 copy.19
  110.1 0.0 copy-done.3
  110.1 0.6 copy.20
Async XLA Ops:
  104.9 1.9 %copy-start.2 = (bf16[512,512]{1,0:T(8,128)(2,1)S(1)}, bf16[512,512]{1,0:T(8,128)(2,1)}, u32[]{:S(2)}) copy-start(bf16[512,512]{1,0:T(8,128)(2,1)} %get-tuple-element.11) | copy-start | bytes 1572868
  106.8 1.2 %copy-start.1 = (bf16[512,512]{1,0:T(8,128)(2,1)S(1)}, bf16[512,512]{1,0:T(8,128)(2,1)}, u32[]{:S(2)}) copy-start(bf16[512,512]{1,0:T(8,128)(2,1)} %get-tuple-element.12) | copy-start | bytes 1572868
  108.1 1.2 %copy-start = (bf16[512,512]{1,0:T(8,128)(2,1)S(1)}, bf16[512,512]{1,0:T(8,128)(2,1)}, u32[]{:S(2)}) copy-start(bf16[512,512]{1,0:T(8,128)(2,1)} %get-tuple-element.13) | copy-start | bytes 1572868
  109.3 0.8 copy-start.3

commit v3 on v2

--- a/solution.py
+++ b/solution.py
@@ -91,21 +91,14 @@
     pl.semaphore_wait(barrier, n - 1)
     for d in range(1, n):
         small_copy(idbuf, id_send, id_recv, d, z).start()
-    @pl.when(z < n - 1)
-    def _():
-        up_copy(0, 0, z + 1).start()
-
-    @pl.when(z > 0)
-    def _():
-        down_copy(0, 0, z - 1).start()
-
-    @pl.when(z == 0)
-    def _():
-        up_copy(1, 0, z + 1).start()
-
-    @pl.when(z == n - 1)
-    def _():
-        down_copy(1, 0, z - 1).start()
+    for kind in range(2):
+        @pl.when(z < n - 1)
+        def _():
+            up_copy(kind, 0, z + 1).start()
+
+        @pl.when(z > 0)
+        def _():
+            down_copy(kind, 0, z - 1).start()
 
     def spread_ids(block):
         row = idbuf[block][0:1, :]
@@ -294,7 +287,7 @@
             jnp.mean(part * part, axis=1, keepdims=True) + 1e-06
         )
 
-    def pass_on(kind, g, seen_up, seen_down):
+    def pass_on(kind, g):
         @pl.when(z >= g)
         def _():
             landed(up_bufs, up_recv, kind, g - 1, z - g, z - 1)
@@ -303,11 +296,6 @@
             def _():
                 up_copy(kind, g, z + 1).start()
 
-        if seen_up:
-            @pl.when((z == g) & (z < n - 1))
-            def _():
-                up_copy(1, 0, z + 1).start()
-
         @pl.when(z + g < n)
         def _():
             landed(down_bufs, down_recv, kind, g - 1, z + g, z + 1)
@@ -316,14 +304,9 @@
             def _():
                 down_copy(kind, g, z - 1).start()
 
-        if seen_down:
-            @pl.when((z + g == n - 1) & (z > 0))
-            def _():
-                down_copy(1, 0, z - 1).start()
-
     pl.when(z == 0)(finish_scores)
     for g in range(1, n):
-        pass_on(0, g, True, True)
+        pass_on(0, g)
 
         @pl.when(z >= g)
         def _():
@@ -333,7 +316,7 @@
     attend_block(z, True)
     pl.when(z == 0)(complete)
     for g in range(1, n):
-        pass_on(1, g, False, False)
+        pass_on(1, g)
 
         @pl.when(z >= g)
         def _():

time: 111 us -> 99.8 us (0.90)
  Pallas kernels: 103 us -> 91.5 us
    pallas_call x1, Pallas kernels: 103 us -> 91.5 us  [dense_body(): pl.pallas_call(functools.partial(dense_kernel, n, clusters, tile), out_sh...]
where the time goes in v3:
time: 99.8 us; the launch traced here: 99.5 us
  Pallas kernels  91.5 us (92%)
  local copies, waits for them, and re-layouts  6.64 us (7%)
    pallas_call x1, Pallas kernels, dense_body(): pl.pallas_call(functools.partial(dense_kernel, n, clusters, tile), out_sh...  91.5 us
    unnamed x13, local copies, waits for them, and re-layouts  5.79 us

profile of v3, /device:TPU:0, one launch (start us, length us, event | category | flops | bytes accessed | tf_op | source)
XLA Modules:
  0.0 99.5 jit_solution(2233319399686070544)
XLA Ops:
  0.6 0.7 convert_element_type.14
  1.3 0.1 broadcast_in_dim.4
  1.4 0.1 convert_element_type.16
  1.6 0.6 broadcast_in_dim.10.ids_ref
  2.2 91.5 %shard_map.101 = (bf16[512,512]{1,0:T(8,128)(2,1)}, bf16[512,512]{1,0:T(8,128)(2,1)}, bf16[512,512]{1,0:T(8,128)(2,1)}, bf16[512,512]{1,0:T(8,128)(2,1)}, f32[8,512]{1,0:T(8,128)}) custom-call(bf16[512,512]{1,0:T(8,128)(2,1)} %q_hbm.1, bf16[512,512]{1,0:T(8,128)(2,1)} %k_hbm.1, bf16[512,512]{1,0:T(8,128)(2,1)} %v_hbm.1, bf16[512,512]{1,0:T(8,128)(2,1)} %g_hbm.1, ...), custom_call_target="tpu_custom_call" | custom-call | tf_op jit(solution)/shard_map/pallas_call | solution.py:373
  93.7 0.0 copy-start.2
  93.7 1.9 %copy.16 = bf16[512,512]{1,0:T(8,128)(2,1)} copy(bf16[512,512]{1,0:T(8,128)(2,1)} %get-tuple-element.10) | data formatting | bytes 1048576
  95.6 0.0 copy-done.2
  95.6 0.0 copy-start.1
  95.6 0.8 copy.17
  96.4 0.4 copy-done.1
  96.8 0.0 copy-start
  96.8 0.8 copy.18
  97.6 0.4 copy-done
  98.1 0.0 copy-start.3
  98.1 0.8 copy.19
  98.9 0.0 copy-done.3
  98.9 0.6 copy.20
Async XLA Ops:
  93.7 1.9 %copy-start.2 = (bf16[512,512]{1,0:T(8,128)(2,1)S(1)}, bf16[512,512]{1,0:T(8,128)(2,1)}, u32[]{:S(2)}) copy-start(bf16[512,512]{1,0:T(8,128)(2,1)} %get-tuple-element.11) | copy-start | bytes 1572868
  95.6 1.2 %copy-start.1 = (bf16[512,512]{1,0:T(8,128)(2,1)S(1)}, bf16[512,512]{1,0:T(8,128)(2,1)}, u32[]{:S(2)}) copy-start(bf16[512,512]{1,0:T(8,128)(2,1)} %get-tuple-element.12) | copy-start | bytes 1572868
  96.8 1.2 %copy-start = (bf16[512,512]{1,0:T(8,128)(2,1)S(1)}, bf16[512,512]{1,0:T(8,128)(2,1)}, u32[]{:S(2)}) copy-start(bf16[512,512]{1,0:T(8,128)(2,1)} %get-tuple-element.13) | copy-start | bytes 1572868
  98.1 0.8 copy-start.3
